TPU v7x, 32 devices: a whole 2x2x4 slice. The times are simulated.
32 devices in a mesh: groups: 2 (over x), row: 16 (over z, y, core).
Axes of the slice: x: 2, y: 2, z: 4, core: 2. Of those that a mesh axis runs over, the one named last changes fastest.
Arguments:
- hblocks: float32 [1024, 6, 128, 128], P(('groups', 'row')), parts along dimension 0, may hold values from -0.21875 to 0.21875
- hcols: int32 [1024, 6], P(('groups', 'row')), parts along dimension 0, may hold values from 0 to 511, as said below
- hmask: int32 [1024, 6], P(('groups', 'row')), parts along dimension 0, may hold values 0 or 1
- tmask: int32 [1024, 2], P('groups'), parts along dimension 0, may hold values from 0 to 1, as said below
- owner: int32 [1024], P('groups'), parts along dimension 0, may hold values from 0 to 15, as said below
- cheb_now: float32 [131072, 256], P(('groups', 'row')), parts along dimension 0, may hold values from -6 to 6
- cheb_prev: float32 [131072, 256], P(('groups', 'row')), parts along dimension 0, may hold values from -6 to 6
Outputs:
- cheb_next: float32 [131072, 256], P(('groups', 'row')), parts along dimension 0
There are 2 independent parts, one for each index of `groups`. A program takes and returns all parts, laid end to end along the dimension named above; each array names one. Nothing has to cross between parts.
Inputs may be any that keep to these rules, and one draw needn't show every extreme that they name: `hcols`: each block row names 6 different block columns, each within 64 block rows of its own in the periodic order. `tmask`: among the block rows of one device at most 32 blocks are occupied, exactly 32 on some device. The block rows of one device go to every owner exactly 2 at a time.
All inputs are finite; a program needn't handle non-finite values. No bound on the sum of `hmask` on one device may be relied on, other than what follows from the above.
Results may differ from a plain program's by a relative error of at most 0.00007.
Values sent between devices are 32-bit elements; how exact they have to be, the bound alone decides.
A program may use at most 192 MiB of HBM per device.

v0:
```python
import functools

import jax
import jax.numpy as jnp
from jax import lax
from jax.experimental import pallas as pl
from jax.experimental.pallas import tpu as pltpu
from jax.sharding import PartitionSpec as P

REACH = 2
WINDOW = 2 * REACH + 1
OCCUPIED = 32
CHUNKS = 8
MESH = pl.DeviceIdType.MESH


def remote(src, dst, send, recv, to):
    return pltpu.make_async_remote_copy(
        src_ref=src, dst_ref=dst, send_sem=send, recv_sem=recv,
        device_id={"row": to}, device_id_type=MESH,
    )


def halo_kernel(n, source_ref, slab_ref, win_ref, packed, near_s, near_r, far_s, far_r, sib_s, sib_r, fwd_s, fwd_r, own_sem):
    me = lax.axis_index("row")
    core = lax.rem(me, 2)
    odd = lax.rem(me // 2, 2)
    partner = me + 2 - 4 * odd
    relay_to = lax.rem(me + 4 - 8 * odd + n, n)
    relay_from = lax.rem(me - 4 + 8 * odd + n, n)
    sibling = me + 1 - 2 * core
    per = OCCUPIED // CHUNKS
    blk = slab_ref.shape[1]

    barrier = pltpu.get_barrier_semaphore()
    for other in (partner, relay_to, relay_from, sibling):
        pl.semaphore_signal(barrier, inc=1, device_id={"row": other}, device_id_type=MESH)
    pl.semaphore_wait(barrier, 4)

    def part(slot, i):
        return win_ref.at[slot, pl.ds(i * per, per)]

    def near(i):
        return remote(packed.at[pl.ds(i * per, per)], part(4 * odd, i), near_s.at[i], near_r.at[i], partner)

    def sib(i):
        return remote(packed.at[pl.ds(i * per, per)], part(1 + 2 * core, i), sib_s.at[i], sib_r.at[i], sibling)

    def far(i):
        return remote(part(4 - 4 * odd, i), part(4 * odd, i), far_s.at[i], far_r.at[i], relay_to)

    def fwd(i):
        return remote(part(4 - 4 * core, i), part(3 - 2 * core, i), fwd_s.at[i], fwd_r.at[i], sibling)

    def arrived(slot, i, sems):
        return remote(part(slot, i), part(slot, i), sems.at[i], sems.at[i], partner)

    def own(i):
        return pltpu.make_async_copy(packed.at[pl.ds(i * per, per)], part(REACH, i), own_sem.at[i])

    for i in range(CHUNKS):
        for j in range(per):
            spot = source_ref[i * per + j]
            rows = slab_ref[spot // 2]
            packed[i * per + j] = jnp.where(lax.rem(spot, 2) == 0, rows[:, :blk], rows[:, blk:])
        near(i).start()
    for i in range(CHUNKS):
        sib(i).start()
        own(i).start()

    for i in range(CHUNKS):
        arrived(4 - 4 * odd, i, near_r).wait_recv()
        far(i).start()

        @pl.when(odd == core)
        def _():
            fwd(i).start()

    for i in range(CHUNKS):
        arrived(4 * odd, i, far_r).wait_recv()

        @pl.when(odd != core)
        def _():
            fwd(i).start()

    for i in range(CHUNKS):
        arrived(3 - 2 * core, i, sib_r).wait_recv()
        arrived(1 + 2 * core, i, fwd_r).wait_recv()
        near(i).wait_send()
        sib(i).wait_send()
        far(i).wait_send()
        fwd(i).wait_send()
        own(i).wait()


def halo(source, slab, n):
    rb, blk, width = slab.shape
    sems = [pltpu.SemaphoreType.DMA((CHUNKS,)) for _ in range(9)]
    return pl.pallas_call(
        functools.partial(halo_kernel, n),
        out_shape=jax.ShapeDtypeStruct((WINDOW, OCCUPIED, blk, blk), jnp.float32),
        in_specs=[pl.BlockSpec(memory_space=pltpu.SMEM), pl.BlockSpec(memory_space=pltpu.VMEM)],
        out_specs=pl.BlockSpec(memory_space=pl.ANY),
        scratch_shapes=[pltpu.VMEM((OCCUPIED, blk, blk), jnp.float32)] + sems,
        compiler_params=pltpu.CompilerParams(collective_id=0, has_side_effects=True, vmem_limit_bytes=32 << 20),
    )(source, slab)


def term_kernel(table_ref, column_ref, place_ref, win_ref, blocks_ref, prev_ref, out_ref, high, low):
    del place_ref
    row = pl.program_id(0)
    slots = blocks_ref.shape[1]
    count = win_ref.shape[0]

    @pl.when(row == 0)
    def _():
        @pl.loop(0, count)
        def _(i):
            x = win_ref[i]
            h = x.astype(jnp.bfloat16)
            high[i] = h
            low[i] = (x - h.astype(jnp.float32)).astype(jnp.bfloat16)

        high[count] = jnp.zeros(high.shape[1:], high.dtype)
        low[count] = jnp.zeros(low.shape[1:], low.dtype)

    total = None
    for pair in range(0, slots, 2):
        a_high, a_low, b_high, b_low = [], [], [], []
        for s in range(pair, min(pair + 2, slots)):
            a = blocks_ref[0, s]
            h = a.astype(jnp.bfloat16)
            a_high.append(h)
            a_low.append((a - h.astype(jnp.float32)).astype(jnp.bfloat16))
            column = column_ref[row * slots + s]
            left, right = table_ref[2 * column], table_ref[2 * column + 1]
            b_high.append(jnp.concatenate([high[left], high[right]], axis=1))
            b_low.append(jnp.concatenate([low[left], low[right]], axis=1))
        a_high, a_low = jnp.concatenate(a_high, axis=1), jnp.concatenate(a_low, axis=1)
        b_high, b_low = jnp.concatenate(b_high, axis=0), jnp.concatenate(b_low, axis=0)
        both = jnp.dot(jnp.concatenate([a_high, a_low], axis=0), b_high, preferred_element_type=jnp.float32)
        rows = a_high.shape[0]
        piece = both[:rows] + both[rows:] + jnp.dot(a_high, b_low, preferred_element_type=jnp.float32)
        total = piece if total is None else total + piece
    out_ref[0] = 2.0 * total - prev_ref[0]


def term(table, column, place, win, blocks, prev):
    rb, slots, blk, _ = blocks.shape
    width = prev.shape[2]
    count = win.shape[0]
    return pl.pallas_call(
        term_kernel,
        out_shape=jax.ShapeDtypeStruct((rb, blk, width), jnp.float32),
        grid_spec=pltpu.PrefetchScalarGridSpec(
            num_scalar_prefetch=3,
            grid=(rb,),
            in_specs=[
                pl.BlockSpec(memory_space=pltpu.VMEM),
                pl.BlockSpec((1, slots, blk, blk), lambda i, t, c, p: (i, 0, 0, 0)),
                pl.BlockSpec((1, blk, width), lambda i, t, c, p: (i, 0, 0)),
            ],
            out_specs=pl.BlockSpec((1, blk, width), lambda i, t, c, p: (p[i], 0, 0)),
            scratch_shapes=[pltpu.VMEM((count + 1, blk, blk), jnp.bfloat16)] * 2,
        ),
        compiler_params=pltpu.CompilerParams(vmem_limit_bytes=48 << 20),
    )(table, column, place, win, blocks, prev)


def exchange_kernel(n, send_ref, out_ref, send_sem, recv_sem, own_sem):
    me = lax.axis_index("row")
    per = send_ref.shape[0] // n
    barrier = pltpu.get_barrier_semaphore()

    @pl.loop(1, n)
    def _(j):
        pl.semaphore_signal(barrier, inc=1, device_id={"row": lax.rem(me + j, n)}, device_id_type=MESH)

    pl.semaphore_wait(barrier, n - 1)

    def copy(j):
        to = lax.rem(me + j, n)
        return remote(
            send_ref.at[pl.ds(to * per, per)], out_ref.at[pl.ds(me * per, per)],
            send_sem.at[j], recv_sem.at[j], to,
        )

    def arrival(j):
        came = lax.rem(me + n - j, n)
        piece = out_ref.at[pl.ds(came * per, per)]
        return remote(piece, piece, send_sem.at[j], recv_sem.at[j], came)

    @pl.loop(1, n)
    def _(j):
        copy(lax.rem(j + n // 2 - 1, n - 1) + 1).start()

    own = pltpu.make_async_copy(
        send_ref.at[pl.ds(me * per, per)], out_ref.at[pl.ds(me * per, per)], own_sem
    )
    own.start()
    own.wait()

    @pl.loop(1, n)
    def _(j):
        copy(j).wait_send()
        arrival(j).wait_recv()


def exchange(send, n):
    return pl.pallas_call(
        functools.partial(exchange_kernel, n),
        out_shape=jax.ShapeDtypeStruct(send.shape, send.dtype),
        in_specs=[pl.BlockSpec(memory_space=pl.ANY)],
        out_specs=pl.BlockSpec(memory_space=pl.ANY),
        scratch_shapes=[
            pltpu.SemaphoreType.DMA((n,)),
            pltpu.SemaphoreType.DMA((n,)),
            pltpu.SemaphoreType.DMA,
        ],
        compiler_params=pltpu.CompilerParams(collective_id=1, has_side_effects=True),
    )(send)


def local(hblocks, hcols, hmask, tmask, owner, cheb_now, cheb_prev):
    n = lax.axis_size("row")
    me = lax.axis_index("row")
    rb, slots, blk, _ = hblocks.shape
    width = cheb_now.shape[1]
    wb = width // blk
    nblocks = rb * n
    per_owner = rb // n
    cells = rb * wb
    zero = WINDOW * OCCUPIED

    iota = jnp.arange(cells, dtype=jnp.int32)
    near = (me - REACH + jnp.arange(WINDOW, dtype=jnp.int32)) % n
    marks = jnp.take(tmask.reshape(n, cells), near, axis=0)
    ahead = (iota[:, None] < iota[None, :]).astype(jnp.int32)
    spot = jnp.sum(marks[:, :, None] * ahead[None], axis=1)
    table = jnp.where(marks == 1, jnp.arange(WINDOW, dtype=jnp.int32)[:, None] * OCCUPIED + spot, zero)
    table = jnp.concatenate([table.reshape(-1), jnp.full((wb,), zero, jnp.int32)])
    hit = (spot[REACH][None, :] == jnp.arange(OCCUPIED, dtype=jnp.int32)[:, None]) & (marks[REACH][None, :] == 1)
    source = jnp.sum(jnp.where(hit, iota[None, :], 0), axis=1)

    relative = (hcols - (me - REACH) * rb) % nblocks
    column = jnp.where(hmask == 1, relative, WINDOW * rb).reshape(-1)

    my_owner = lax.dynamic_slice_in_dim(owner, me * rb, rb, 0)
    row = jnp.arange(rb, dtype=jnp.int32)
    earlier = (my_owner[:, None] == my_owner[None, :]) & (row[None, :] < row[:, None])
    place = my_owner * per_owner + jnp.sum(earlier.astype(jnp.int32), axis=1)

    win = halo(source, cheb_now.reshape(rb, blk, width), n)
    send = term(
        table, column, place, win.reshape(zero, blk, blk), hblocks, cheb_prev.reshape(rb, blk, width)
    )
    return exchange(send, n).reshape(rb * blk, width)


def solution(mesh):
    in_specs = (
        P(("groups", "row"), None, None, None),
        P(("groups", "row"), None),
        P(("groups", "row"), None),
        P("groups", None),
        P("groups"),
        P(("groups", "row"), None),
        P(("groups", "row"), None),
    )
    out_specs = P(("groups", "row"), None)
    return jax.shard_map(local, mesh=mesh, in_specs=in_specs, out_specs=out_specs, check_vma=False)
```

profile of v0, /device:TPU:0, one launch (start us, length us, event | category | flops | bytes accessed | tf_op | source)
XLA Modules:
  0.0 201.6 jit_solution(14994538217920580072)
XLA Ops:
  0.0 0.8 dynamic_slice.3
  0.8 0.2 convert_reduce_fusion
  1.0 0.8 multiply_add_fusion.place_ref
  1.7 0.7 fusion.4
  2.5 0.1 copy.12
  2.6 0.1 reshape.121.column_ref
  2.7 0.8 copy.11
  3.5 0.2 reshape.120
  3.7 0.6 gather_fusion
  4.2 0.1 broadcast_select_fusion
  4.3 0.1 multiply_reduce_fusion
  4.4 0.1 add_select_fusion.1
  4.5 0.1 select_n.75
  4.6 0.1 select_reduce_fusion.source_ref
  4.7 0.0 copy-start.2
  4.7 2.2 %copy-done.2 = f32[4096,256]{1,0:T(8,128)S(1)} copy-done((f32[4096,256]{1,0:T(8,128)S(1)}, f32[4096,256]{1,0:T(8,128)}, u32[]{:S(2)}) %copy-start.2) | copy-done | bytes 4194328
  6.9 60.2 %shard_map.73 = f32[5,32,128,128]{3,2,1,0:T(8,128)S(1)} custom-call(s32[32]{0:T(128)S(1)} %select_reduce_fusion.source_ref, f32[32,128,256]{2,1,0:T(8,128)S(1)} %bitcast.11), custom_call_target="tpu_custom_call" | custom-call | tf_op jit(solution)/shard_map/pallas_call | solution.py:99
  67.1 0.0 copy-start
  67.1 4.0 %copy-done = f32[5,32,128,128]{3,2,1,0:T(8,128)} copy-done((f32[5,32,128,128]{3,2,1,0:T(8,128)}, f32[5,32,128,128]{3,2,1,0:T(8,128)S(1)}, u32[]{:S(2)}) %copy-start) | copy-done | bytes 10485784
  71.1 28.4 %shard_map.74.send_ref = f32[32,128,256]{2,1,0:T(8,128)S(1)} custom-call(s32[322]{0:T(512)S(1)} %concatenate.3.table_ref, s32[192]{0:T(256)S(1)} %reshape.121.column_ref, s32[32]{0:T(128)S(1)} %multiply_add_fusion.place_ref, f32[160,128,128]{2,1,0:T(8,128)} %bitcast.10, f32[32,6,128,128]{3,2,1,0:T(8,128)} %blocks_ref.1, f32[32,128,256]{2,1,0:T(8,128)} %bitcast.13), custom_call_target="tpu_custom_call" | custom-call | tf_op jit(solution)/shard_map/pallas_call | solution.py:152
  99.5 0.0 copy-start.1
  99.5 2.0 copy-done.1
  101.5 95.6 %shard_map.75 = f32[32,128,256]{2,1,0:T(8,128)} custom-call(f32[32,128,256]{2,1,0:T(8,128)} %copy-done.1), custom_call_target="tpu_custom_call" | custom-call | tf_op jit(solution)/shard_map/pallas_call | solution.py:210
  197.1 4.5 %copy.14 = f32[4096,256]{1,0:T(8,128)} copy(f32[4096,256]{1,0:T(8,128)} %bitcast.12) | data formatting | bytes 8388608
  (8 shorter events, 0.1 us)
Async XLA Ops:
  4.7 2.2 %copy-start.2 = (f32[4096,256]{1,0:T(8,128)S(1)}, f32[4096,256]{1,0:T(8,128)}, u32[]{:S(2)}) copy-start(f32[4096,256]{1,0:T(8,128)} %param.12) | copy-start | bytes 12582916
  67.1 4.0 %copy-start = (f32[5,32,128,128]{3,2,1,0:T(8,128)}, f32[5,32,128,128]{3,2,1,0:T(8,128)S(1)}, u32[]{:S(2)}) copy-start(f32[5,32,128,128]{3,2,1,0:T(8,128)S(1)} %shard_map.73) | copy-start | bytes 31457284
  99.5 2.0 copy-start.1
where the time goes:
time: 202 us
  Pallas kernels  184 us (91%)
  local copies, waits for them, and re-layouts  15.2 us (8%)
  other arithmetic  2.09 us (1%)
    pallas_call x1, Pallas kernels, exchange(): pl.pallas_call(functools.partial(exchange_kernel, n), out_shape=jax.Shape...  95.6 us
    pallas_call x1, Pallas kernels, halo(): pl.pallas_call(functools.partial(halo_kernel, n), out_shape=jax.ShapeDtyp...  60.2 us
    pallas_call x1, Pallas kernels, term(): pl.pallas_call(term_kernel, out_shape=jax.ShapeDtypeStruct((rb, blk, widt...  28.4 us
    unnamed x8, local copies, waits for them, and re-layouts  13.5 us

commit v1 on v0

v1 whole, which is shorter than its diff:
```python
import functools

import jax
import jax.numpy as jnp
from jax import lax
from jax.experimental import pallas as pl
from jax.experimental.pallas import tpu as pltpu
from jax.sharding import PartitionSpec as P

REACH = 2
WINDOW = 2 * REACH + 1
OCCUPIED = 32
CHUNKS = 16
MESH = pl.DeviceIdType.MESH


def remote(src, dst, send, recv, to):
    return pltpu.make_async_remote_copy(
        src_ref=src, dst_ref=dst, send_sem=send, recv_sem=recv,
        device_id={"row": to}, device_id_type=MESH,
    )


def partner_of(me, m, n):
    if n & (n - 1):
        return lax.rem(me + m, n), lax.rem(me + n - m, n)
    to = me
    bit = 1
    while bit < n:
        to = to + lax.rem(m // bit, 2) * (bit - 2 * bit * lax.rem(me // bit, 2))
        bit *= 2
    return to, to


def split(x):
    high = x.astype(jnp.bfloat16)
    return high, (x - high.astype(jnp.float32)).astype(jnp.bfloat16)


def term_kernel(
    n, source_ref, table_ref, column_ref, inverse_ref, slab_hbm, blocks_hbm, prev_hbm, out_ref,
    slab, blocks, prev, packed, win, high, low, stage,
    near_s, near_r, far_s, far_r, sib_s, sib_r, fwd_s, fwd_r, send_sem, recv_sem, load_sem,
):
    me = lax.axis_index("row")
    core = lax.rem(me, 2)
    odd = lax.rem(me // 2, 2)
    partner = me + 2 - 4 * odd
    relay_to = lax.rem(me + 4 - 8 * odd + n, n)
    sibling = me + 1 - 2 * core
    chunk = OCCUPIED // CHUNKS
    rb, slots, blk, _ = blocks.shape
    per = rb // n
    zero = WINDOW * OCCUPIED

    slab_load = pltpu.make_async_copy(slab_hbm, slab, load_sem.at[0])
    blocks_load = pltpu.make_async_copy(blocks_hbm, blocks, load_sem.at[1])
    prev_load = pltpu.make_async_copy(prev_hbm, prev, load_sem.at[2])
    slab_load.start()

    barrier = pltpu.get_barrier_semaphore()

    @pl.loop(1, n)
    def _(j):
        pl.semaphore_signal(barrier, inc=1, device_id={"row": lax.rem(me + j, n)}, device_id_type=MESH)

    slab_load.wait()
    blocks_load.start()
    prev_load.start()
    pl.semaphore_wait(barrier, n - 1)

    def piece(i):
        return packed.at[pl.ds(i * chunk, chunk)]

    def part(slot, i):
        return win.at[pl.ds(slot * OCCUPIED + i * chunk, chunk)]

    def near(i):
        return remote(piece(i), part(4 * odd, i), near_s.at[i], near_r.at[i], partner)

    def sib(i):
        return remote(piece(i), part(1 + 2 * core, i), sib_s.at[i], sib_r.at[i], sibling)

    def far(i):
        return remote(part(4 - 4 * odd, i), part(4 * odd, i), far_s.at[i], far_r.at[i], relay_to)

    def fwd(i):
        return remote(part(4 - 4 * core, i), part(3 - 2 * core, i), fwd_s.at[i], fwd_r.at[i], sibling)

    def arrived(slot, i, sems):
        return remote(part(slot, i), part(slot, i), sems.at[i], sems.at[i], partner)

    def halve(slot, i):
        for k in range(chunk):
            at = slot * OCCUPIED + i * chunk + k
            high[at], low[at] = split(win[at])

    @pl.loop(0, CHUNKS)
    def _(i):
        for k in range(chunk):
            spot = source_ref[i * chunk + k]
            rows = slab[spot // 2]
            packed[i * chunk + k] = jnp.where(lax.rem(spot, 2) == 0, rows[:, :blk], rows[:, blk:])
        near(i).start()

    @pl.loop(0, CHUNKS)
    def _(i):
        sib(i).start()
        for k in range(chunk):
            at = i * chunk + k
            high[REACH * OCCUPIED + at], low[REACH * OCCUPIED + at] = split(packed[at])

    high[zero] = jnp.zeros((blk, blk), jnp.bfloat16)
    low[zero] = jnp.zeros((blk, blk), jnp.bfloat16)

    @pl.loop(0, CHUNKS)
    def _(i):
        arrived(4 - 4 * odd, i, near_r).wait_recv()
        far(i).start()

        @pl.when(odd == core)
        def _():
            fwd(i).start()

        halve(4 - 4 * odd, i)
        arrived(3 - 2 * core, i, sib_r).wait_recv()
        halve(3 - 2 * core, i)

    @pl.loop(0, CHUNKS)
    def _(i):
        arrived(4 * odd, i, far_r).wait_recv()

        @pl.when(odd != core)
        def _():
            fwd(i).start()

        halve(4 * odd, i)

    blocks_load.wait()
    prev_load.wait()

    @pl.loop(0, CHUNKS)
    def _(i):
        arrived(1 + 2 * core, i, fwd_r).wait_recv()
        halve(1 + 2 * core, i)

    def copy(m):
        to, _ = partner_of(me, m, n)
        return remote(
            stage.at[pl.ds(m * per, per)], out_ref.at[pl.ds(me * per, per)],
            send_sem.at[m], recv_sem.at[m], to,
        )

    def arrival(m):
        _, came = partner_of(me, m, n)
        rows = out_ref.at[pl.ds(came * per, per)]
        return remote(rows, rows, send_sem.at[m], recv_sem.at[m], came)

    def compute(m, r):
        to, _ = partner_of(me, m, n)
        row = inverse_ref[to * per + r]
        total = None
        for pair in range(0, slots, 2):
            a_high, a_low, b_high, b_low = [], [], [], []
            for s in range(pair, min(pair + 2, slots)):
                h, l = split(blocks[row, s])
                a_high.append(h)
                a_low.append(l)
                column = column_ref[row * slots + s]
                left, right = table_ref[2 * column], table_ref[2 * column + 1]
                b_high.append(jnp.concatenate([high[left], high[right]], axis=1))
                b_low.append(jnp.concatenate([low[left], low[right]], axis=1))
            a_high, a_low = jnp.concatenate(a_high, axis=1), jnp.concatenate(a_low, axis=1)
            b_high, b_low = jnp.concatenate(b_high, axis=0), jnp.concatenate(b_low, axis=0)
            both = jnp.dot(jnp.concatenate([a_high, a_low], axis=0), b_high, preferred_element_type=jnp.float32)
            add = both[:blk] + both[blk:] + jnp.dot(a_high, b_low, preferred_element_type=jnp.float32)
            total = add if total is None else total + add
        stage[m * per + r] = 2.0 * total - prev[row]

    @pl.loop(0, n - 1)
    def _(j):
        m = n - 1 - j
        @pl.loop(0, per)
        def _(r):
            compute(m, r)

        copy(m).start()

    @pl.loop(0, per)
    def _(r):
        compute(0, r)

    own = pltpu.make_async_copy(stage.at[pl.ds(0, per)], out_ref.at[pl.ds(me * per, per)], load_sem.at[3])
    own.start()

    @pl.loop(0, CHUNKS)
    def _(i):
        near(i).wait_send()
        sib(i).wait_send()
        far(i).wait_send()
        fwd(i).wait_send()

    own.wait()

    @pl.loop(0, n - 1)
    def _(j):
        m = n - 1 - j
        copy(m).wait_send()
        arrival(m).wait_recv()


def term(source, table, column, inverse, slab, blocks, prev, n):
    rb, _, blk, _ = blocks.shape
    width = prev.shape[2]
    count = WINDOW * OCCUPIED
    smem = pl.BlockSpec(memory_space=pltpu.SMEM)
    hbm = pl.BlockSpec(memory_space=pl.ANY)
    return pl.pallas_call(
        functools.partial(term_kernel, n),
        out_shape=jax.ShapeDtypeStruct((rb, blk, width), jnp.float32),
        in_specs=[smem] * 4 + [hbm] * 3,
        out_specs=hbm,
        scratch_shapes=[
            pltpu.VMEM(slab.shape, jnp.float32),
            pltpu.VMEM(blocks.shape, jnp.float32),
            pltpu.VMEM(prev.shape, jnp.float32),
            pltpu.VMEM((OCCUPIED, blk, blk), jnp.float32),
            pltpu.VMEM((count, blk, blk), jnp.float32),
            pltpu.VMEM((count + 1, blk, blk), jnp.bfloat16),
            pltpu.VMEM((count + 1, blk, blk), jnp.bfloat16),
            pltpu.VMEM(prev.shape, jnp.float32),
        ]
        + [pltpu.SemaphoreType.DMA((CHUNKS,)) for _ in range(8)]
        + [pltpu.SemaphoreType.DMA((n,))] * 2
        + [pltpu.SemaphoreType.DMA((4,))],
        compiler_params=pltpu.CompilerParams(collective_id=0, has_side_effects=True, vmem_limit_bytes=56 << 20),
    )(source, table, column, inverse, slab, blocks, prev)


def local(hblocks, hcols, hmask, tmask, owner, cheb_now, cheb_prev):
    n = lax.axis_size("row")
    me = lax.axis_index("row")
    rb, slots, blk, _ = hblocks.shape
    width = cheb_now.shape[1]
    wb = width // blk
    nblocks = rb * n
    per_owner = rb // n
    cells = rb * wb
    zero = WINDOW * OCCUPIED

    iota = jnp.arange(cells, dtype=jnp.int32)
    near = (me - REACH + jnp.arange(WINDOW, dtype=jnp.int32)) % n
    marks = jnp.take(tmask.reshape(n, cells), near, axis=0)
    ahead = (iota[:, None] < iota[None, :]).astype(jnp.int32)
    spot = jnp.sum(marks[:, :, None] * ahead[None], axis=1)
    table = jnp.where(marks == 1, jnp.arange(WINDOW, dtype=jnp.int32)[:, None] * OCCUPIED + spot, zero)
    table = jnp.concatenate([table.reshape(-1), jnp.full((wb,), zero, jnp.int32)])
    hit = (spot[REACH][None, :] == jnp.arange(OCCUPIED, dtype=jnp.int32)[:, None]) & (marks[REACH][None, :] == 1)
    source = jnp.sum(jnp.where(hit, iota[None, :], 0), axis=1)

    relative = (hcols - (me - REACH) * rb) % nblocks
    column = jnp.where(hmask == 1, relative, WINDOW * rb).reshape(-1)

    my_owner = lax.dynamic_slice_in_dim(owner, me * rb, rb, 0)
    row = jnp.arange(rb, dtype=jnp.int32)
    earlier = (my_owner[:, None] == my_owner[None, :]) & (row[None, :] < row[:, None])
    place = my_owner * per_owner + jnp.sum(earlier.astype(jnp.int32), axis=1)

    inverse = jnp.sum(jnp.where(place[None, :] == row[:, None], row[None, :], 0), axis=1)

    out = term(
        source, table, column, inverse,
        cheb_now.reshape(rb, blk, width), hblocks, cheb_prev.reshape(rb, blk, width), n,
    )
    return out.reshape(rb * blk, width)


def solution(mesh):
    in_specs = (
        P(("groups", "row"), None, None, None),
        P(("groups", "row"), None),
        P(("groups", "row"), None),
        P("groups", None),
        P("groups"),
        P(("groups", "row"), None),
        P(("groups", "row"), None),
    )
    out_specs = P(("groups", "row"), None)
    return jax.shard_map(local, mesh=mesh, in_specs=in_specs, out_specs=out_specs, check_vma=False)
```

time: 202 us -> 171 us (0.85)
  Pallas kernels: 184 us -> 159 us
  local copies, waits for them, and re-layouts: 15.2 us -> 8.2 us
    pallas_call x3 -> x1, Pallas kernels: 184 us -> 159 us  [term(): pl.pallas_call(functools.partial(term_kernel, n), out_shape=jax.ShapeDtyp...]
    unnamed x8 -> x2, local copies, waits for them, and re-layouts: 13.5 us -> 5.3 us
where the time goes in v1:
time: 171 us; the launch traced here: 170 us
  Pallas kernels  159 us (93%)
  local copies, waits for them, and re-layouts  8.2 us (5%)
  other arithmetic  3.34 us (2%)
    pallas_call x1, Pallas kernels, term(): pl.pallas_call(functools.partial(term_kernel, n), out_shape=jax.ShapeDtyp...  159 us
    unnamed x2, local copies, waits for them, and re-layouts  5.3 us

profile of v1, /device:TPU:0, one launch (start us, length us, event | category | flops | bytes accessed | tf_op | source)
XLA Modules:
  0.0 170.1 jit_solution(545586405898718186)
XLA Ops:
  0.0 0.8 dynamic_slice.3
  0.8 0.2 convert_reduce_fusion
  1.0 0.8 multiply_add_fusion
  1.7 0.7 select_reduce_fusion.inverse_ref
  2.5 0.7 fusion.4
  3.2 0.1 copy.12
  3.3 0.7 reshape.119.column_ref
  3.9 0.8 copy.11
  4.8 0.2 reshape.118
  4.9 0.6 gather_fusion
  5.5 0.1 broadcast_select_fusion
  5.6 0.1 multiply_reduce_fusion
  5.7 0.1 add_select_fusion.1
  5.8 0.1 select_n.80
  5.9 0.7 select_reduce_fusion.1.source_ref
  6.5 0.6 concatenate.3.table_ref
  7.1 158.5 %shard_map.73 = f32[32,128,256]{2,1,0:T(8,128)} custom-call(s32[32]{0:T(128)} %select_reduce_fusion.1.source_ref, s32[322]{0:T(512)} %concatenate.3.table_ref, s32[192]{0:T(256)} %reshape.119.column_ref, s32[32]{0:T(128)} %select_reduce_fusion.inverse_ref, f32[32,128,256]{2,1,0:T(8,128)} %bitcast.10, f32[32,6,128,128]{3,2,1,0:T(8,128)} %blocks_hbm.1, ...), custom_call_target="tpu_custom_call" | custom-call | tf_op jit(solution)/shard_map/pallas_call | solution.py:218
  165.6 4.5 %copy.14 = f32[4096,256]{1,0:T(8,128)} copy(f32[4096,256]{1,0:T(8,128)} %bitcast.9) | data formatting | bytes 8388608
  (7 shorter events, 0.1 us)

commit v2 on v1

--- a/solution.py
+++ b/solution.py
@@ -38,8 +38,8 @@
 
 
 def term_kernel(
-    n, source_ref, table_ref, column_ref, inverse_ref, slab_hbm, blocks_hbm, prev_hbm, out_ref,
-    slab, blocks, prev, packed, win, high, low, stage,
+    n, marks_ref, column_ref, owner_ref, slab_hbm, blocks_hbm, prev_hbm, out_ref,
+    slab, blocks, prev, packed, win, high, low, stage, table_ref,
     near_s, near_r, far_s, far_r, sib_s, sib_r, fwd_s, fwd_r, send_sem, recv_sem, load_sem,
 ):
     me = lax.axis_index("row")
@@ -52,6 +52,8 @@
     rb, slots, blk, _ = blocks.shape
     per = rb // n
     zero = WINDOW * OCCUPIED
+    wb = slab.shape[2] // blk
+    span = WINDOW * rb + 1
 
     slab_load = pltpu.make_async_copy(slab_hbm, slab, load_sem.at[0])
     blocks_load = pltpu.make_async_copy(blocks_hbm, blocks, load_sem.at[1])
@@ -95,12 +97,32 @@
             at = slot * OCCUPIED + i * chunk + k
             high[at], low[at] = split(win[at])
 
+    def mark(device, c, r):
+        return marks_ref[c * n * rb + device * rb + r]
+
+    def occupied(which):
+        seen, spot = 0, 0
+        for c in range(wb):
+            for r in range(rb):
+                hit = mark(me, c, r)
+                spot = jnp.where((hit == 1) & (seen == which), c * rb + r, spot)
+                seen = seen + hit
+        return spot
+
+    def owned(to, rank):
+        seen, row = 0, 0
+        for b in range(rb):
+            hit = owner_ref[me * rb + b] == to
+            row = jnp.where(hit & (seen == rank), b, row)
+            seen = seen + hit.astype(jnp.int32)
+        return row
+
     @pl.loop(0, CHUNKS)
     def _(i):
         for k in range(chunk):
-            spot = source_ref[i * chunk + k]
-            rows = slab[spot // 2]
-            packed[i * chunk + k] = jnp.where(lax.rem(spot, 2) == 0, rows[:, :blk], rows[:, blk:])
+            spot = occupied(i * chunk + k)
+            rows = slab[lax.rem(spot, rb)]
+            packed[i * chunk + k] = jnp.where(spot < rb, rows[:, :blk], rows[:, blk:])
         near(i).start()
 
     @pl.loop(0, CHUNKS)
@@ -112,6 +134,20 @@
 
     high[zero] = jnp.zeros((blk, blk), jnp.bfloat16)
     low[zero] = jnp.zeros((blk, blk), jnp.bfloat16)
+
+    @pl.loop(0, WINDOW)
+    def _(w):
+        device = lax.rem(me + w - REACH + n, n)
+
+        seen = 0
+        for c in range(wb):
+            for r in range(rb):
+                hit = mark(device, c, r)
+                table_ref[c * span + w * rb + r] = jnp.where(hit == 1, w * OCCUPIED + seen, zero)
+                seen = seen + hit
+
+    for c in range(wb):
+        table_ref[c * span + WINDOW * rb] = zero
 
     @pl.loop(0, CHUNKS)
     def _(i):
@@ -158,7 +194,7 @@
 
     def compute(m, r):
         to, _ = partner_of(me, m, n)
-        row = inverse_ref[to * per + r]
+        row = owned(to, r)
         total = None
         for pair in range(0, slots, 2):
             a_high, a_low, b_high, b_low = [], [], [], []
@@ -166,8 +202,8 @@
                 h, l = split(blocks[row, s])
                 a_high.append(h)
                 a_low.append(l)
-                column = column_ref[row * slots + s]
-                left, right = table_ref[2 * column], table_ref[2 * column + 1]
+                column = column_ref[s * rb + row]
+                left, right = table_ref[column], table_ref[span + column]
                 b_high.append(jnp.concatenate([high[left], high[right]], axis=1))
                 b_low.append(jnp.concatenate([low[left], low[right]], axis=1))
             a_high, a_low = jnp.concatenate(a_high, axis=1), jnp.concatenate(a_low, axis=1)
@@ -209,7 +245,7 @@
         arrival(m).wait_recv()
 
 
-def term(source, table, column, inverse, slab, blocks, prev, n):
+def term(marks, column, owner, slab, blocks, prev, n):
     rb, _, blk, _ = blocks.shape
     width = prev.shape[2]
     count = WINDOW * OCCUPIED
@@ -218,7 +254,7 @@
     return pl.pallas_call(
         functools.partial(term_kernel, n),
         out_shape=jax.ShapeDtypeStruct((rb, blk, width), jnp.float32),
-        in_specs=[smem] * 4 + [hbm] * 3,
+        in_specs=[smem] * 3 + [hbm] * 3,
         out_specs=hbm,
         scratch_shapes=[
             pltpu.VMEM(slab.shape, jnp.float32),
@@ -229,12 +265,13 @@
             pltpu.VMEM((count + 1, blk, blk), jnp.bfloat16),
             pltpu.VMEM((count + 1, blk, blk), jnp.bfloat16),
             pltpu.VMEM(prev.shape, jnp.float32),
+            pltpu.SMEM((width // blk * (WINDOW * rb + 1),), jnp.int32),
         ]
         + [pltpu.SemaphoreType.DMA((CHUNKS,)) for _ in range(8)]
         + [pltpu.SemaphoreType.DMA((n,))] * 2
         + [pltpu.SemaphoreType.DMA((4,))],
-        compiler_params=pltpu.CompilerParams(collective_id=0, has_side_effects=True, vmem_limit_bytes=56 << 20),
-    )(source, table, column, inverse, slab, blocks, prev)
+        compiler_params=pltpu.CompilerParams(collective_id=0, has_side_effects=True, vmem_limit_bytes=49 << 20),
+    )(marks, column, owner, slab, blocks, prev)
 
 
 def local(hblocks, hcols, hmask, tmask, owner, cheb_now, cheb_prev):
@@ -242,34 +279,10 @@
     me = lax.axis_index("row")
     rb, slots, blk, _ = hblocks.shape
     width = cheb_now.shape[1]
-    wb = width // blk
-    nblocks = rb * n
-    per_owner = rb // n
-    cells = rb * wb
-    zero = WINDOW * OCCUPIED
-
-    iota = jnp.arange(cells, dtype=jnp.int32)
-    near = (me - REACH + jnp.arange(WINDOW, dtype=jnp.int32)) % n
-    marks = jnp.take(tmask.reshape(n, cells), near, axis=0)
-    ahead = (iota[:, None] < iota[None, :]).astype(jnp.int32)
-    spot = jnp.sum(marks[:, :, None] * ahead[None], axis=1)
-    table = jnp.where(marks == 1, jnp.arange(WINDOW, dtype=jnp.int32)[:, None] * OCCUPIED + spot, zero)
-    table = jnp.concatenate([table.reshape(-1), jnp.full((wb,), zero, jnp.int32)])
-    hit = (spot[REACH][None, :] == jnp.arange(OCCUPIED, dtype=jnp.int32)[:, None]) & (marks[REACH][None, :] == 1)
-    source = jnp.sum(jnp.where(hit, iota[None, :], 0), axis=1)
-
-    relative = (hcols - (me - REACH) * rb) % nblocks
-    column = jnp.where(hmask == 1, relative, WINDOW * rb).reshape(-1)
-
-    my_owner = lax.dynamic_slice_in_dim(owner, me * rb, rb, 0)
-    row = jnp.arange(rb, dtype=jnp.int32)
-    earlier = (my_owner[:, None] == my_owner[None, :]) & (row[None, :] < row[:, None])
-    place = my_owner * per_owner + jnp.sum(earlier.astype(jnp.int32), axis=1)
-
-    inverse = jnp.sum(jnp.where(place[None, :] == row[:, None], row[None, :], 0), axis=1)
-
+    relative = (hcols - (me - REACH) * rb) % (rb * n)
+    column = jnp.where(hmask == 1, relative, WINDOW * rb).T.reshape(-1)
     out = term(
-        source, table, column, inverse,
+        tmask.T.reshape(-1), column, owner,
         cheb_now.reshape(rb, blk, width), hblocks, cheb_prev.reshape(rb, blk, width), n,
     )
     return out.reshape(rb * blk, width)

time: 171 us -> 165 us (0.965)
  local copies, waits for them, and re-layouts: 8.2 us -> 3.46 us
  other arithmetic: 3.34 us -> 0.71 us
  Pallas kernels: 159 us -> 161 us
    pallas_call x1, Pallas kernels: 159 us -> 161 us  [term(): pl.pallas_call(functools.partial(term_kernel, n), out_shape=jax.ShapeDtyp...]
    unnamed x2 -> x4, local copies, waits for them, and re-layouts: 5.3 us -> 3.39 us
where the time goes in v2:
time: 165 us
  Pallas kernels  161 us (98%)
  local copies, waits for them, and re-layouts  3.46 us (2%)
    pallas_call x1, Pallas kernels, term(): pl.pallas_call(functools.partial(term_kernel, n), out_shape=jax.ShapeDtyp...  161 us
    unnamed x4, local copies, waits for them, and re-layouts  3.39 us

profile of v2, /device:TPU:0, one launch (start us, length us, event | category | flops | bytes accessed | tf_op | source)
XLA Modules:
  0.0 165.0 jit_solution(12811628916576363795)
XLA Ops:
  0.0 0.7 fusion.2
  0.7 0.1 reshape.16.column_ref
  0.8 0.7 copy.8
  1.5 0.0 copy-start
  1.5 0.7 copy-done
  2.2 160.8 %shard_map.73 = f32[32,128,256]{2,1,0:T(8,128)S(1)} custom-call(s32[1024]{0:T(1024)S(1)} %bitcast.9, s32[192]{0:T(256)S(1)} %reshape.16.column_ref, s32[512]{0:T(512)S(1)} %copy-done, f32[32,128,256]{2,1,0:T(8,128)} %bitcast.10, f32[32,6,128,128]{3,2,1,0:T(8,128)} %blocks_hbm.1, f32[32,128,256]{2,1,0:T(8,128)} %bitcast.11), custom_call_target="tpu_custom_call" | custom-call | tf_op jit(solution)/shard_map/pallas_call | solution.py:254
  163.0 2.0 %copy.10 = f32[4096,256]{1,0:T(8,128)} copy(f32[4096,256]{1,0:T(8,128)S(1)} %bitcast.8) | data formatting | bytes 8388608
Async XLA Ops:
  1.5 0.7 copy-start

commit v3 on v2

--- a/solution.py
+++ b/solution.py
@@ -101,13 +101,14 @@
         return marks_ref[c * n * rb + device * rb + r]
 
     def occupied(which):
-        seen, spot = 0, 0
+        seen, spots = 0, [0] * chunk
         for c in range(wb):
             for r in range(rb):
                 hit = mark(me, c, r)
-                spot = jnp.where((hit == 1) & (seen == which), c * rb + r, spot)
+                for k in range(chunk):
+                    spots[k] = jnp.where((hit == 1) & (seen == which + k), c * rb + r, spots[k])
                 seen = seen + hit
-        return spot
+        return spots
 
     def owned(to, rank):
         seen, row = 0, 0
@@ -119,24 +120,16 @@
 
     @pl.loop(0, CHUNKS)
     def _(i):
-        for k in range(chunk):
-            spot = occupied(i * chunk + k)
+        for k, spot in enumerate(occupied(i * chunk)):
             rows = slab[lax.rem(spot, rb)]
             packed[i * chunk + k] = jnp.where(spot < rb, rows[:, :blk], rows[:, blk:])
         near(i).start()
-
-    @pl.loop(0, CHUNKS)
-    def _(i):
         sib(i).start()
-        for k in range(chunk):
-            at = i * chunk + k
-            high[REACH * OCCUPIED + at], low[REACH * OCCUPIED + at] = split(packed[at])
 
     high[zero] = jnp.zeros((blk, blk), jnp.bfloat16)
     low[zero] = jnp.zeros((blk, blk), jnp.bfloat16)
 
-    @pl.loop(0, WINDOW)
-    def _(w):
+    def note(w):
         device = lax.rem(me + w - REACH + n, n)
 
         seen = 0
@@ -157,6 +150,14 @@
         @pl.when(odd == core)
         def _():
             fwd(i).start()
+
+        for k in range(chunk):
+            at = i * chunk + k
+            high[REACH * OCCUPIED + at], low[REACH * OCCUPIED + at] = split(packed[at])
+
+        @pl.when(i < WINDOW)
+        def _():
+            note(i)
 
         halve(4 - 4 * odd, i)
         arrived(3 - 2 * core, i, sib_r).wait_recv()

time: 165 us -> 164 us (level)
  Pallas kernels: 161 us -> 159 us
where the time goes in v3:
time: 164 us
  Pallas kernels  159 us (97%)
  local copies, waits for them, and re-layouts  3.46 us (2%)
    pallas_call x1, Pallas kernels, term(): pl.pallas_call(functools.partial(term_kernel, n), out_shape=jax.ShapeDtyp...  159 us
    unnamed x4, local copies, waits for them, and re-layouts  3.39 us

profile of v3, /device:TPU:0, one launch (start us, length us, event | category | flops | bytes accessed | tf_op | source)
XLA Modules:
  0.0 163.6 jit_solution(5001280556528873473)
XLA Ops:
  0.0 0.7 fusion.2
  0.7 0.1 reshape.16.column_ref
  0.8 0.7 copy.8
  1.5 0.0 copy-start
  1.5 0.7 copy-done
  2.2 159.4 %shard_map.73 = f32[32,128,256]{2,1,0:T(8,128)S(1)} custom-call(s32[1024]{0:T(1024)S(1)} %bitcast.9, s32[192]{0:T(256)S(1)} %reshape.16.column_ref, s32[512]{0:T(512)S(1)} %copy-done, f32[32,128,256]{2,1,0:T(8,128)} %bitcast.10, f32[32,6,128,128]{3,2,1,0:T(8,128)} %blocks_hbm.1, f32[32,128,256]{2,1,0:T(8,128)} %bitcast.11), custom_call_target="tpu_custom_call" | custom-call | tf_op jit(solution)/shard_map/pallas_call | solution.py:255
  161.6 2.0 %copy.10 = f32[4096,256]{1,0:T(8,128)} copy(f32[4096,256]{1,0:T(8,128)S(1)} %bitcast.8) | data formatting | bytes 8388608
Async XLA Ops:
  1.5 0.7 copy-start
